TPU v7x, 32 devices: a whole 2x2x4 slice. The times are simulated.
32 devices in a mesh: half: 2 (over core), dp: 8 (over z, x), mp: 2 (over y).
Axes of the slice: x: 2, y: 2, z: 4, core: 2. Of those that a mesh axis runs over, the one named last changes fastest.
Arguments:
- tokens: bfloat16 [2, 16384, 768], P('half', ('dp', 'mp')), may hold values from -6 to 6
- norm_gains: float32 [2, 2, 768], P('half'), may hold values from 0.5 to 1.5
- qkv_w: bfloat16 [2, 768, 3, 768], P('half', None, None, 'mp'), may hold values from -0.21875 to 0.21875
- out_w: bfloat16 [2, 768, 768], P('half', None, 'mp'), may hold values from -0.875 to 0.875
- up_w: bfloat16 [2, 768, 3072], P('half', None, 'mp'), may hold values from -0.21875 to 0.21875
- down_w: bfloat16 [2, 768, 3072], P('half', None, 'mp'), may hold values from -0.109375 to 0.109375
- memory: bfloat16 [2, 4096, 4, 768], P('half', 'dp'), may hold values from -12 to 12
- memory_ids: int32 [256, 10], P(('dp', 'mp')), may hold values from 0 to 4095, as said below
- counts: int32 [256], P(('dp', 'mp')), may hold values from 1 to 10, 1536 in all
- prefix_mask: int32 [256, 20], P(('dp', 'mp')), may hold values 0 or 1
- cotangent: bfloat16 [2, 16384, 768], P('half', ('dp', 'mp')), may hold values from -6 to 6
Outputs:
- activations: bfloat16 [2, 16384, 768], P('half', ('dp', 'mp'))
- input_grad: float32 [2, 16384, 768], P('half', ('dp', 'mp'))
- score_grads: float32 [256, 10], P(('dp', 'mp'))
- gain_grads: float32 [2, 2, 768], P('half')
- qkv_grads: float32 [2, 768, 3, 768], P('half', 'dp', None, 'mp')
- out_grads: float32 [2, 768, 768], P('half', 'dp', 'mp')
- up_grads: float32 [2, 768, 3072], P('half', 'dp', 'mp')
- down_grads: float32 [2, 768, 3072], P('half', 'dp', 'mp')
Inputs may be any that keep to these rules, and one draw needn't show every extreme that they name: memory_ids[q, j] // 512 = (i + t * 10 + j) mod 8, where q is the t-th of the 16 questions held by a device whose dp index is i.
All inputs are finite; a program needn't handle non-finite values. No bound on the sum of `counts` or of `prefix_mask` on one device may be relied on, other than what follows from the above.
Results may differ from a plain program's by a relative error of at most 0.017.
Values may be sent and summed in bfloat16 or wider, within the bound.
No kernel may reach another device: no remote copies, remote signals or barrier semaphores. Data moves between devices by JAX's collectives and lax.ppermute only.
A program may use at most 320 MiB of HBM per device.

v0:
```python
import jax
import jax.numpy as jnp
from jax import lax
from jax.sharding import PartitionSpec as P

HDIM = 64
QLEN = 64
MB = 4


NORM_EPS = 1e-06
MASKED_BIAS = -30000.0
HIGHEST_MODE = lax.Precision.HIGHEST


def passed_along(value, axis, steps):
    count = lax.axis_size(axis)
    initial, last = (max(0, -steps), min(count, count - steps))
    return lax.ppermute(value, axis, [(source, source + steps) for source in range(initial, last)])


def rms_norm(row_block, gain_vec):
    return (
        row_block
        * lax.rsqrt(jnp.mean(row_block * row_block, axis=-1, keepdims=True) + NORM_EPS)
        * gain_vec
    )


def gelu_tanh(pre_act):
    return jax.nn.gelu(pre_act, approximate=True)


def head_sum(partial_sum):
    return lax.psum_scatter(
        partial_sum.astype(jnp.bfloat16), "mp", scatter_dimension=0, tiled=True
    ).astype(jnp.float32)


def grad_rows(grad_low):
    return lax.all_gather(grad_low, "mp", axis=0, tiled=True)


def reduce_grads(matrices, gain_part):
    shards = (
        lax.psum_scatter(matrices[0], "dp", scatter_dimension=0, tiled=True),
        lax.psum_scatter(matrices[1], "dp", scatter_dimension=0, tiled=True),
        lax.psum_scatter(matrices[2], "dp", scatter_dimension=0, tiled=True),
        lax.psum_scatter(matrices[3], "dp", scatter_dimension=0, tiled=True),
    )
    gain_total = lax.psum(gain_part, ("dp", "mp"))
    return (shards, gain_total)


def add_trees(first_tree, second_tree):
    if first_tree is None:
        return second_tree
    return jax.tree.map(jnp.add, first_tree, second_tree)


def select_block(stack_arr, block_index):
    return lax.dynamic_index_in_dim(stack_arr, block_index, 0, keepdims=False)


def store_block(stack_arr, new_block, block_index, valid_now):
    previous = select_block(stack_arr, block_index)
    chosen = jnp.where(valid_now, new_block, previous)
    return lax.dynamic_update_index_in_dim(stack_arr, chosen, block_index, 0)


def attn_logits(queries, keys_self, keys_pref, bias_slots):
    head_scale = HDIM ** (-0.5)
    self_part = (
        jnp.einsum("nthe,nshe->nhts", queries, keys_self, preferred_element_type=jnp.float32)
        * head_scale
    )
    pref_part = (
        jnp.einsum("nthe,nshe->nhts", queries, keys_pref, preferred_element_type=jnp.float32)
        * head_scale
    )
    return (self_part, pref_part + bias_slots.astype(jnp.float32)[:, None, None, :])


def body(
    tokens,
    norm_gains,
    qkv_w,
    out_w,
    up_w,
    down_w,
    memory,
    memory_ids,
    counts,
    prefix_mask,
    cotangent,
):
    half_index = lax.axis_index("half")
    joining_side = half_index == 1
    shard_count = lax.axis_size("dp")
    shard_index = lax.axis_index("dp")
    tok_dev = tokens.shape[1]
    model_width = tokens.shape[2]
    q_dev, k_most = memory_ids.shape
    rows_mb = tok_dev // MB
    quest_mb = q_dev // MB
    mem_dev = memory.shape[1]
    score_scale = (4 * model_width) ** (-0.5)
    head_scale = HDIM ** (-0.5)
    qkv_mat = qkv_w[0]
    out_mat = out_w[0]
    up_mat = up_w[0]
    down_mat = down_w[0]
    split_count = lax.axis_size("mp")
    local_hd = qkv_mat.shape[2]
    head_count = local_hd // HDIM
    local_ff = up_mat.shape[1]
    group_count = split_count * quest_mb
    rows_all = split_count * rows_mb
    slot_total = q_dev * k_most
    capacity = (slot_total + shard_count - 1) // shard_count
    local_rows = jnp.concatenate(
        [
            memory_ids.reshape(-1) % mem_dev,
            jnp.zeros((capacity * shard_count - slot_total,), jnp.int32),
        ]
    )
    requests = jnp.roll(local_rows.reshape(capacity, shard_count), shard_index, axis=1).T
    table_half = memory[0]
    answers = lax.all_to_all(
        table_half[lax.all_to_all(requests, "dp", split_axis=0, concat_axis=0, tiled=True)],
        "dp",
        split_axis=0,
        concat_axis=0,
        tiled=True,
    )
    answers = jnp.roll(jnp.swapaxes(answers, 0, 1), -shard_index, axis=1)
    own_found = answers.reshape(capacity * shard_count, 4, model_width)[:slot_total].reshape(
        q_dev, k_most, 4, model_width
    )
    key_blocks = own_found.reshape(MB, quest_mb, k_most, 4, model_width)
    prefixes = lax.all_to_all(own_found, "mp", split_axis=3, concat_axis=0, tiled=True)
    prefix_blocks = jnp.moveaxis(
        prefixes.reshape(split_count, MB, quest_mb, k_most, 4, local_hd), 1, 0
    )
    prefix_blocks = prefix_blocks.reshape(MB, group_count, k_most, 4, local_hd)
    slot_valid = (
        (jnp.arange(k_most)[None, :] < counts[:, None])[:, :, None]
        & (prefix_mask.reshape(q_dev, k_most, 2) == 1)
        & joining_side
    )
    slot_valid = slot_valid.reshape(MB, quest_mb, 2 * k_most)
    token_blocks = tokens[0].reshape(MB, rows_mb, model_width)
    cot_blocks = cotangent[0].reshape(MB, rows_mb, model_width)
    gain_one = norm_gains[0, 0]
    gain_two = norm_gains[0, 1]
    kept_normed = jnp.zeros((MB, rows_all, model_width), jnp.bfloat16)
    kept_proj = jnp.zeros((MB, rows_all, 3, local_hd), jnp.bfloat16)
    kept_mixed = jnp.zeros((MB, rows_all, local_hd), jnp.bfloat16)
    kept_logtot = jnp.zeros((MB, group_count, head_count, QLEN), jnp.float32)
    kept_bias = jnp.zeros((MB, group_count, 2 * k_most), jnp.bfloat16)
    kept_resid = jnp.zeros((MB, rows_mb, model_width), jnp.float32)
    kept_normed_two = jnp.zeros((MB, rows_all, model_width), jnp.bfloat16)
    kept_pre = jnp.zeros((MB, rows_all, local_ff), jnp.float32)
    kept_result = jnp.zeros((MB, rows_mb, model_width), jnp.float32)

    def split_heads(flat_rows):
        return flat_rows.reshape(group_count, QLEN, head_count, HDIM)

    incoming = jnp.zeros((quest_mb, k_most), jnp.bfloat16)
    for step_no in range(MB + 1):
        raw_index = step_no - half_index
        valid_now = (raw_index >= 0) & (raw_index < MB)
        block_index = jnp.clip(raw_index, 0, MB - 1)
        row_block = select_block(token_blocks, block_index).astype(jnp.float32)
        normed = rms_norm(row_block, gain_one).astype(jnp.bfloat16)
        bias_own = jnp.where(
            select_block(slot_valid, block_index),
            jnp.repeat(incoming.astype(jnp.float32), 2, axis=1),
            MASKED_BIAS,
        ).astype(jnp.bfloat16)
        normed_all, bias_all = (
            lax.all_gather(normed, "mp", axis=0, tiled=True),
            lax.all_gather(bias_own, "mp", axis=0, tiled=True),
        )
        projected = jnp.einsum(
            "td,dch->tch", normed_all, qkv_mat, preferred_element_type=jnp.float32
        ).astype(jnp.bfloat16)
        pref_block = select_block(prefix_blocks, block_index)
        keys_pref = pref_block[:, :, 0:2].reshape(group_count, 2 * k_most, head_count, HDIM)
        values_pref = pref_block[:, :, 2:4].reshape(group_count, 2 * k_most, head_count, HDIM)
        queries = split_heads(projected[:, 0])
        values_self = split_heads(projected[:, 2])
        self_part, pref_part = attn_logits(
            queries, split_heads(projected[:, 1]), keys_pref, bias_all
        )
        row_top = jnp.maximum(jnp.max(self_part, axis=-1), jnp.max(pref_part, axis=-1))
        self_exp = jnp.exp(self_part - row_top[..., None])
        pref_exp = jnp.exp(pref_part - row_top[..., None])
        exp_total = jnp.sum(self_exp, axis=-1) + jnp.sum(pref_exp, axis=-1)
        log_total = row_top + jnp.log(exp_total)
        self_prob = (self_exp / exp_total[..., None]).astype(jnp.bfloat16)
        pref_prob = (pref_exp / exp_total[..., None]).astype(jnp.bfloat16)
        mixed_heads = jnp.einsum(
            "nhts,nshe->nthe", self_prob, values_self, preferred_element_type=jnp.float32
        ) + jnp.einsum(
            "nhts,nshe->nthe", pref_prob, values_pref, preferred_element_type=jnp.float32
        )
        mixed_heads = mixed_heads.astype(jnp.bfloat16).reshape(rows_all, local_hd)
        attn_own = head_sum(
            jnp.einsum("th,dh->td", mixed_heads, out_mat, preferred_element_type=jnp.float32)
        )
        residual = row_block + attn_own
        normed_two = rms_norm(residual, gain_two).astype(jnp.bfloat16)
        normed_two_all = lax.all_gather(normed_two, "mp", axis=0, tiled=True)
        hidden_pre = jnp.einsum(
            "td,df->tf", normed_two_all, up_mat, preferred_element_type=jnp.float32
        )
        hidden = gelu_tanh(hidden_pre).astype(jnp.bfloat16)
        ff_own = head_sum(
            jnp.einsum("tf,df->td", hidden, down_mat, preferred_element_type=jnp.float32)
        )
        result = residual + ff_own
        pooled = jnp.mean(result.reshape(quest_mb, 4, QLEN // 4, model_width), axis=2)
        mem_keys = select_block(key_blocks, block_index).astype(jnp.float32)
        scores = jnp.einsum("ncd,njcd->nj", pooled, mem_keys, precision=HIGHEST_MODE) * score_scale
        incoming = passed_along(scores.astype(jnp.bfloat16), "half", 1)
        kept_normed = store_block(kept_normed, normed_all, block_index, valid_now)
        kept_proj = store_block(kept_proj, projected, block_index, valid_now)
        kept_mixed = store_block(kept_mixed, mixed_heads, block_index, valid_now)
        kept_logtot = store_block(kept_logtot, log_total, block_index, valid_now)
        kept_bias = store_block(kept_bias, bias_all, block_index, valid_now)
        kept_resid = store_block(kept_resid, residual, block_index, valid_now)
        kept_normed_two = store_block(kept_normed_two, normed_two_all, block_index, valid_now)
        kept_pre = store_block(kept_pre, hidden_pre, block_index, valid_now)
        kept_result = store_block(kept_result, result, block_index, valid_now)
    kept_input_grad = jnp.zeros((MB, rows_mb, model_width), jnp.float32)
    kept_score = jnp.zeros((MB, quest_mb, k_most), jnp.float32)
    score_in = jnp.zeros((quest_mb, k_most), jnp.bfloat16)
    reduced = None
    summed = None
    for step_no in range(MB + 1):
        raw_index = MB - step_no - half_index
        valid_now = (raw_index >= 0) & (raw_index < MB)
        block_index = jnp.clip(raw_index, 0, MB - 1)
        mem_keys = select_block(key_blocks, block_index).astype(jnp.float32)
        pooled_grad = (
            jnp.einsum(
                "nj,njcd->ncd", score_in.astype(jnp.float32), mem_keys, precision=HIGHEST_MODE
            )
            * score_scale
        )
        spread_grad = jnp.broadcast_to(
            (pooled_grad / (QLEN // 4))[:, :, None, :], (quest_mb, 4, QLEN // 4, model_width)
        ).reshape(rows_mb, model_width)
        result_grad = select_block(cot_blocks, block_index).astype(jnp.float32) + spread_grad
        result_all = grad_rows(result_grad.astype(jnp.bfloat16))
        hidden_pre = select_block(kept_pre, block_index)
        hidden = gelu_tanh(hidden_pre).astype(jnp.bfloat16)
        down_grad = jnp.einsum("td,tf->df", result_all, hidden, preferred_element_type=jnp.float32)
        hidden_grad = jnp.einsum(
            "td,df->tf", result_all, down_mat, preferred_element_type=jnp.float32
        )
        gelu_value, gelu_back = jax.vjp(gelu_tanh, hidden_pre)
        pre_low = gelu_back(hidden_grad)[0].astype(jnp.bfloat16)
        normed_two_all = select_block(kept_normed_two, block_index)
        up_grad = jnp.einsum(
            "td,tf->df", normed_two_all, pre_low, preferred_element_type=jnp.float32
        )
        two_part = jnp.einsum("tf,df->td", pre_low, up_mat, preferred_element_type=jnp.float32)
        normed_two_grad = lax.psum_scatter(
            two_part.astype(jnp.bfloat16), "mp", scatter_dimension=0, tiled=True
        ).astype(jnp.float32)
        residual = select_block(kept_resid, block_index)
        norm_value, norm_back = jax.vjp(rms_norm, residual, gain_two)
        resid_part, gain_two_grad = norm_back(normed_two_grad)
        residual_grad = result_grad + resid_part
        attn_all = grad_rows(residual_grad.astype(jnp.bfloat16))
        mixed_heads = select_block(kept_mixed, block_index)
        out_grad = jnp.einsum(
            "td,th->dh", attn_all, mixed_heads, preferred_element_type=jnp.float32
        )
        mixed_low = jnp.einsum(
            "td,dh->th", attn_all, out_mat, preferred_element_type=jnp.float32
        ).astype(jnp.bfloat16)
        mixed_low = split_heads(mixed_low)
        projected = select_block(kept_proj, block_index)
        pref_block = select_block(prefix_blocks, block_index)
        keys_pref = pref_block[:, :, 0:2].reshape(group_count, 2 * k_most, head_count, HDIM)
        values_pref = pref_block[:, :, 2:4].reshape(group_count, 2 * k_most, head_count, HDIM)
        queries = split_heads(projected[:, 0])
        keys_self = split_heads(projected[:, 1])
        values_self = split_heads(projected[:, 2])
        self_part, pref_part = attn_logits(
            queries, keys_self, keys_pref, select_block(kept_bias, block_index)
        )
        log_total = select_block(kept_logtot, block_index)
        self_prob = jnp.exp(self_part - log_total[..., None])
        pref_prob = jnp.exp(pref_part - log_total[..., None])
        self_dp = jnp.einsum(
            "nthe,nshe->nhts", mixed_low, values_self, preferred_element_type=jnp.float32
        )
        pref_dp = jnp.einsum(
            "nthe,nshe->nhts", mixed_low, values_pref, preferred_element_type=jnp.float32
        )
        row_delta = jnp.sum(self_prob * self_dp, axis=-1) + jnp.sum(pref_prob * pref_dp, axis=-1)
        self_dl = self_prob * (self_dp - row_delta[..., None])
        pref_dl = pref_prob * (pref_dp - row_delta[..., None])
        query_grad = (
            jnp.einsum(
                "nhts,nshe->nthe", self_dl, keys_self.astype(jnp.float32), precision=HIGHEST_MODE
            )
            + jnp.einsum(
                "nhts,nshe->nthe", pref_dl, keys_pref.astype(jnp.float32), precision=HIGHEST_MODE
            )
        ) * head_scale
        key_grad = (
            jnp.einsum(
                "nhts,nthe->nshe", self_dl, queries.astype(jnp.float32), precision=HIGHEST_MODE
            )
            * head_scale
        )
        value_grad = jnp.einsum(
            "nhts,nthe->nshe",
            self_prob.astype(jnp.bfloat16),
            mixed_low,
            preferred_element_type=jnp.float32,
        )
        qkv_low = jnp.stack(
            [
                query_grad.reshape(rows_all, local_hd),
                key_grad.reshape(rows_all, local_hd),
                value_grad.reshape(rows_all, local_hd),
            ],
            axis=1,
        ).astype(jnp.bfloat16)
        normed_all = select_block(kept_normed, block_index)
        qkv_grad = jnp.einsum(
            "td,tch->dch", normed_all, qkv_low, preferred_element_type=jnp.float32
        )
        slot_grad = jnp.sum(pref_dl, axis=(1, 2)).reshape(group_count, k_most, 2).sum(axis=-1)
        input_term = jnp.einsum("tch,dch->td", qkv_low, qkv_mat, preferred_element_type=jnp.float32)
        normed_grad, score_part = (
            lax.psum_scatter(
                input_term.astype(jnp.bfloat16), "mp", scatter_dimension=0, tiled=True
            ).astype(jnp.float32),
            lax.psum_scatter(
                slot_grad.astype(jnp.bfloat16), "mp", scatter_dimension=0, tiled=True
            ).astype(jnp.float32),
        )
        row_block = select_block(token_blocks, block_index).astype(jnp.float32)
        first_value, first_back = jax.vjp(rms_norm, row_block, gain_one)
        input_part, gain_one_grad = first_back(normed_grad)
        input_now = residual_grad + input_part
        score_low = score_part.astype(jnp.bfloat16)
        score_now = jnp.where(joining_side, score_low, score_in).astype(jnp.float32)
        kept_input_grad = store_block(kept_input_grad, input_now, block_index, valid_now)
        kept_score = store_block(kept_score, score_now, block_index, valid_now)
        score_in = passed_along(score_low, "half", -1)
        local_mats = tuple(
            (
                jnp.where(valid_now, piece_grad, 0.0)
                for piece_grad in (qkv_grad, out_grad, up_grad, down_grad)
            )
        )
        local_gain = jnp.where(valid_now, jnp.stack([gain_one_grad, gain_two_grad]), 0.0)
        summed = add_trees(summed, (local_mats, local_gain))
    reduced = reduce_grads(summed[0], summed[1])
    mat_shards, gain_total = reduced
    activations = kept_result.reshape(tok_dev, model_width).astype(jnp.bfloat16)[None]
    input_grad = kept_input_grad.reshape(tok_dev, model_width)[None]
    score_grads = kept_score.reshape(q_dev, k_most)
    return (
        activations,
        input_grad,
        score_grads,
        gain_total[None],
        mat_shards[0][None],
        mat_shards[1][None],
        mat_shards[2][None],
        mat_shards[3][None],
    )


def solution(mesh):
    placed = (
        P("half", ("dp", "mp"), None),
        P("half", None, None),
        P("half", None, None, "mp"),
        P("half", None, "mp"),
        P("half", None, "mp"),
        P("half", None, "mp"),
        P("half", "dp", None, None),
        P(("dp", "mp"), None),
        P(("dp", "mp")),
        P(("dp", "mp"), None),
        P("half", ("dp", "mp"), None),
    )
    return jax.shard_map(
        body,
        mesh=mesh,
        in_specs=placed,
        out_specs=(
            P("half", ("dp", "mp"), None),
            P("half", ("dp", "mp"), None),
            P(("dp", "mp"), None),
            P("half", None, None),
            P("half", "dp", None, "mp"),
            P("half", "dp", "mp"),
            P("half", "dp", "mp"),
            P("half", "dp", "mp"),
        ),
        check_vma=False,
    )
```

profile of v0, /device:TPU:17, one launch (start us, length us, event | category | flops | bytes accessed | tf_op | source)
XLA Modules:
  0.0 1480.4 jit_solution(10744528592024645816)
XLA Ops:
  26.5 8.9 all_gather.75
  51.5 7.7 copy.994
  59.2 11.1 reshape.995
  83.7 8.4 reshape.996
  92.1 10.7 copy.995
  117.4 22.2 %reduce-scatter.25.cloned.1.call-done = bf16[256,768]{1,0:T(8,128)(2,1)} async-done(((bf16[512,768]{1,0:T(8,128)(2,1)}), bf16[256,768]{1,0:T(8,128)(2,1)}) %reduce-scatter.25.cloned.1.call-update) | async-done | bytes 393232 | tf_op jit(solution)/shard_map/reduce_scatter | solution.py:35
  143.4 10.8 all_gather.77
  171.3 18.3 %all_gather.78 = bf16[512,768]{1,0:T(8,128)(2,1)S(1)} all-gather(bf16[256,768]{1,0:T(8,128)(2,1)} %get-tuple-element.97), channel_id=1, replica_groups=mesh['half'=2,'dp'=8,'mp'=2] {'mp'}, dimensions={0}, use_global_device_ids=true | all-gather | bytes 1179648 | tf_op jit(solution)/shard_map/all_gather | solution.py:182
  225.1 16.1 %reduce-scatter.29.cloned.1.call-done = bf16[256,768]{1,0:T(8,128)(2,1)} async-done(((bf16[512,768]{1,0:T(8,128)(2,1)}), bf16[256,768]{1,0:T(8,128)(2,1)}) %reduce-scatter.29.cloned.1.call-update) | async-done | bytes 393232 | tf_op jit(solution)/shard_map/reduce_scatter | solution.py:35
  243.9 10.7 all_gather.80
  267.3 15.8 %all_gather.81 = bf16[512,768]{1,0:T(8,128)(2,1)S(1)} all-gather(bf16[256,768]{1,0:T(8,128)(2,1)S(1)} %get-tuple-element.95), channel_id=1, replica_groups=mesh['half'=2,'dp'=8,'mp'=2] {'mp'}, dimensions={0}, use_global_device_ids=true | all-gather | bytes 1179648 | tf_op jit(solution)/shard_map/all_gather | solution.py:182
  321.9 15.1 %reduce-scatter.33.cloned.1.call-done = bf16[256,768]{1,0:T(8,128)(2,1)} async-done(((bf16[512,768]{1,0:T(8,128)(2,1)}), bf16[256,768]{1,0:T(8,128)(2,1)}) %reduce-scatter.33.cloned.1.call-update) | async-done | bytes 393232 | tf_op jit(solution)/shard_map/reduce_scatter | solution.py:35
  340.4 10.7 all_gather.83
  367.2 17.6 %all_gather.84 = bf16[512,768]{1,0:T(8,128)(2,1)S(1)} all-gather(bf16[256,768]{1,0:T(8,128)(2,1)S(1)} %copy-done.165), channel_id=1, replica_groups=mesh['half'=2,'dp'=8,'mp'=2] {'mp'}, dimensions={0}, use_global_device_ids=true | all-gather | bytes 1179648 | tf_op jit(solution)/shard_map/all_gather | solution.py:182
  416.5 9.2 all_gather.90
  441.1 7.5 all_gather.86
  478.0 9.8 reduce-scatter.39.cloned.1.call-done
  493.5 7.6 collective-permute-done.3
  536.6 10.7 all_gather.89
  599.4 10.8 all_gather.91
  637.5 11.1 all_gather.92
  685.3 10.2 all_gather.93
  726.4 11.5 all_gather.94
  777.5 11.3 all_gather.95
  819.4 11.5 all_gather.96
  877.8 11.2 all_gather.97
  919.5 11.5 all_gather.98
  1058.7 17.8 %all_gather.99 = bf16[512,768]{1,0:T(8,128)(2,1)S(1)} all-gather(bf16[256,768]{1,0:T(8,128)(2,1)S(1)} %get-tuple-element.58), channel_id=1, replica_groups=mesh['half'=2,'dp'=8,'mp'=2] {'mp'}, dimensions={0}, use_global_device_ids=true | all-gather | bytes 1179648 | tf_op jit(solution)/shard_map/all_gather | solution.py:41
  1176.7 26.7 %psum.7 = f32[1,2,768]{2,1,0:T(2,128)} all-reduce(f32[1,2,768]{2,1,0:T(2,128)S(1)} %fusion.654), channel_id=1, replica_groups=mesh['half'=2,'dp'=8,'mp'=2] {'dp','mp'}, use_global_device_ids=true, to_apply=%region_104.105 | all-reduce | flops 1536 | bytes 12288 | tf_op jit(solution)/shard_map/psum | solution.py:51
  1218.3 56.2 %reduce-scatter.65.cloned.1.call-done = f32[96,3,384]{2,0,1:T(8,128)} async-done(((f32[768,3,384]{2,0,1:T(8,128)}), f32[96,3,384]{2,0,1:T(8,128)}) %reduce-scatter.65.cloned.1.call-update) | async-done | bytes 442384 | tf_op jit(solution)/shard_map/reduce_scatter | solution.py:46
  1274.5 99.3 %reduce-scatter.69.cloned.1.call-done = f32[96,1536]{1,0:T(8,128)} async-done(((f32[768,1536]{1,0:T(8,128)}), f32[96,1536]{1,0:T(8,128)}) %reduce-scatter.69.cloned.1.call-update) | async-done | bytes 589840 | tf_op jit(solution)/shard_map/reduce_scatter | solution.py:48
  1373.8 99.3 %reduce-scatter.71.cloned.1.call-done = f32[96,1536]{1,0:T(8,128)} async-done(((f32[768,1536]{1,0:T(8,128)}), f32[96,1536]{1,0:T(8,128)}) %reduce-scatter.71.cloned.1.call-update) | async-done | bytes 589840 | tf_op jit(solution)/shard_map/reduce_scatter | solution.py:49
  (1208 shorter events, 843.7 us)
Async XLA Ops:
  8.9 8.7 all-to-all-start
  20.3 29.5 %all-to-all-start.1 = ((bf16[8,20,4,768]{3,2,1,0:T(4,128)(2,1)}), bf16[8,20,4,768]{3,2,1,0:T(4,128)(2,1)S(1)}, u32[]{:S(2)}, u32[]{:S(2)}) async-start(bf16[8,20,4,768]{3,2,1,0:T(4,128)(2,1)} %bitcast.1309), calls=%async_computation.1 | async-start | bytes 1966080 | tf_op jit(solution)/shard_map/all_to_all | solution.py:129
  70.3 13.4 all-to-all-start.2
  75.2 64.4 %reduce-scatter.25.cloned.1.call-start = ((), (), s32[]{:S(2)}) async-start(), calls=%async_computation.27 | async-start | bytes 1179648 | tf_op jit(solution)/shard_map/reduce_scatter | solution.py:35
  117.3 83.8 %reduce-scatter.27.cloned.1.call-start = ((), (), s32[]{:S(2)}) async-start(), calls=%async_computation.28 | async-start | bytes 1179648 | tf_op jit(solution)/shard_map/reduce_scatter | solution.py:35
  166.3 74.9 %reduce-scatter.29.cloned.1.call-start = ((), (), s32[]{:S(2)}) async-start(), calls=%async_computation.29 | async-start | bytes 1179648 | tf_op jit(solution)/shard_map/reduce_scatter | solution.py:35
  221.3 72.9 %reduce-scatter.31.cloned.1.call-start = ((), (), s32[]{:S(2)}) async-start(), calls=%async_computation.30 | async-start | bytes 1179648 | tf_op jit(solution)/shard_map/reduce_scatter | solution.py:35
  262.9 74.1 %reduce-scatter.33.cloned.1.call-start = ((), (), s32[]{:S(2)}) async-start(), calls=%async_computation.31 | async-start | bytes 1179648 | tf_op jit(solution)/shard_map/reduce_scatter | solution.py:35
  297.4 6.8 collective-permute-start.1
  316.8 79.2 %reduce-scatter.35.cloned.1.call-start = ((), (), s32[]{:S(2)}) async-start(), calls=%async_computation.32 | async-start | bytes 1179648 | tf_op jit(solution)/shard_map/reduce_scatter | solution.py:35
  359.3 78.3 %reduce-scatter.37.cloned.1.call-start = ((), (), s32[]{:S(2)}) async-start(), calls=%async_computation.33 | async-start | bytes 1179648 | tf_op jit(solution)/shard_map/reduce_scatter | solution.py:35
  415.2 72.6 %reduce-scatter.39.cloned.1.call-start = ((), (), s32[]{:S(2)}) async-start(), calls=%async_computation.34 | async-start | bytes 1179648 | tf_op jit(solution)/shard_map/reduce_scatter | solution.py:35
  456.9 77.2 %reduce-scatter.41.cloned.1.call-start = ((), (), s32[]{:S(2)}) async-start(), calls=%async_computation.35 | async-start | bytes 1179648 | tf_op jit(solution)/shard_map/reduce_scatter | solution.py:35
  489.8 11.3 collective-permute-start.3
  514.3 70.8 %reduce-scatter.43.cloned.1.call-start = ((), (), s32[]{:S(2)}) async-start(), calls=%async_computation.36 | async-start | bytes 1179648 | tf_op jit(solution)/shard_map/reduce_scatter | solution.py:35
  555.6 38.2 %reduce-scatter.45.cloned.1.call-start = ((), (), s32[]{:S(2)}) async-start(), calls=%async_computation.37 | async-start | bytes 1179648 | tf_op jit(solution)/shard_map/reduce_scatter | solution.py:270
  571.9 109.1 %reduce-scatter.49.cloned.1.call-start = ((), (), s32[]{:S(2)}) async-start(), calls=%async_computation.39 | async-start | bytes 1179648 | tf_op jit(solution)/shard_map/reduce_scatter | solution.py:270
  656.9 116.3 %reduce-scatter.53.cloned.1.call-start = ((), (), s32[]{:S(2)}) async-start(), calls=%async_computation.41 | async-start | bytes 1179648 | tf_op jit(solution)/shard_map/reduce_scatter | solution.py:270
  716.4 7.6 collective-permute-start.5
  746.2 127.3 %reduce-scatter.57.cloned.1.call-start = ((), (), s32[]{:S(2)}) async-start(), calls=%async_computation.43 | async-start | bytes 1179648 | tf_op jit(solution)/shard_map/reduce_scatter | solution.py:270
  810.2 6.7 collective-permute-start.6
  839.2 215.3 %reduce-scatter.61.cloned.1.call-start = ((), (), s32[]{:S(2)}) async-start(), calls=%async_computation.45 | async-start | bytes 1179648 | tf_op jit(solution)/shard_map/reduce_scatter | solution.py:270
  910.3 6.8 collective-permute-start.7
  939.3 233.3 %reduce-scatter.47.cloned.1.call-start = ((), (), s32[]{:S(2)}) async-start(), calls=%async_computation.38 | async-start | bytes 1179648 | tf_op jit(solution)/shard_map/reduce_scatter | solution.py:343
  961.3 211.3 %reduce-scatter.51.cloned.1.call-start = ((), (), s32[]{:S(2)}) async-start(), calls=%async_computation.40 | async-start | bytes 1179648 | tf_op jit(solution)/shard_map/reduce_scatter | solution.py:343
  993.0 179.6 %reduce-scatter.55.cloned.1.call-start = ((), (), s32[]{:S(2)}) async-start(), calls=%async_computation.42 | async-start | bytes 1179648 | tf_op jit(solution)/shard_map/reduce_scatter | solution.py:343
  1024.4 148.2 %reduce-scatter.59.cloned.1.call-start = ((), (), s32[]{:S(2)}) async-start(), calls=%async_computation.44 | async-start | bytes 1179648 | tf_op jit(solution)/shard_map/reduce_scatter | solution.py:343
  1054.4 118.2 %reduce-scatter.63.cloned.1.call-start = ((), (), s32[]{:S(2)}) async-start(), calls=%async_computation.46 | async-start | bytes 1179648 | tf_op jit(solution)/shard_map/reduce_scatter | solution.py:343
  1103.9 114.4 %reduce-scatter.67.cloned.1.call-start = ((), (), s32[]{:S(2)}) async-start(), calls=%async_computation.48 | async-start | bytes 1327104 | tf_op jit(solution)/shard_map/reduce_scatter | solution.py:47
  1112.9 161.6 %reduce-scatter.65.cloned.1.call-start = ((), (), s32[]{:S(2)}) async-start(), calls=%async_computation.47 | async-start | bytes 3981312 | tf_op jit(solution)/shard_map/reduce_scatter | solution.py:46
  1123.7 250.1 %reduce-scatter.69.cloned.1.call-start = ((), (), s32[]{:S(2)}) async-start(), calls=%async_computation.49 | async-start | bytes 5308416 | tf_op jit(solution)/shard_map/reduce_scatter | solution.py:48
  1140.8 332.3 %reduce-scatter.71.cloned.1.call-start = ((), (), s32[]{:S(2)}) async-start(), calls=%async_computation.50 | async-start | bytes 5308416 | tf_op jit(solution)/shard_map/reduce_scatter | solution.py:49
  (296 other events, 2441.0 us)
Sparse Core Ops, SparseCore 0:
  117.4 22.1 reduce-scatter.24
  166.4 25.8 reduce-scatter.26
  221.4 19.7 reduce-scatter.28
  263.0 25.4 reduce-scatter.30
  316.9 20.0 reduce-scatter.32
  359.5 23.7 reduce-scatter.34
  415.3 22.3 reduce-scatter.36
  457.0 30.7 reduce-scatter.38
  514.4 19.6 reduce-scatter.40
  555.7 18.2 reduce-scatter.42
  576.3 17.4 reduce-scatter.44
  657.0 17.9 reduce-scatter.48
  746.4 17.3 reduce-scatter.52
  839.3 17.3 reduce-scatter.56
  939.4 17.4 reduce-scatter.60
  961.4 17.4 reduce-scatter.46
  993.1 17.4 reduce-scatter.50
  1024.5 17.4 reduce-scatter.54
  1054.5 25.3 reduce-scatter.58
  1104.0 19.9 reduce-scatter.62
  1128.0 61.6 reduce-scatter.66
  1193.9 80.5 reduce-scatter.64
  1278.7 95.0 reduce-scatter.68
  1377.9 95.1 reduce-scatter.70
where the time goes:
time: 1500 us; the launch traced here: 1480 us
  local copies, waits for them, and re-layouts  383 us (26%)
  waiting for transfers between devices  347 us (23%)
  blocking collectives  297 us (20%)
  matrix products  279 us (19%)
  other arithmetic  112 us (7%)
  starting transfers between devices  43.3 us (3%)
  between operations  19.6 us (1%)
    all_gather x10, blocking collectives, grad_rows(): return lax.all_gather(grad_low, 'mp', axis=0, tiled=True)  116 us
    reduce_scatter x1, waiting for transfers between devices, reduce_grads(): lax.psum_scatter(matrices[2], 'dp', scatter_dimension=0, tiled=True)  99.3 us
    reduce_scatter x1, waiting for transfers between devices, reduce_grads(): lax.psum_scatter(matrices[3], 'dp', scatter_dimension=0, tiled=True)  99.3 us
    reduce_scatter x10, waiting for transfers between devices, head_sum(): lax.psum_scatter(partial_sum.astype(jnp.bfloat16), 'mp', scatter_dimensio...  68.2 us
    all_gather x5, blocking collectives, body(): lax.all_gather(normed, 'mp', axis=0, tiled=True)  67.9 us
    unnamed x599, local copies, waits for them, and re-layouts  66.2 us
    dynamic_slice x39, local copies, waits for them, and re-layouts, select_block(): return lax.dynamic_index_in_dim(stack_arr, block_index, 0, keepdims=False)  65.5 us
    another operation x35, local copies, waits for them, and re-layouts, body(): jnp.stack([query_grad.reshape(rows_all, local_hd), key_grad.reshape(rows_...  64.5 us
  transfers between devices with their start and end apart: 35, of which 16 were waited for; matrix products, arithmetic and copies ran while one was open for 31% of the time, Pallas kernels for 0%

commit v1 on v0

v1 whole, which is shorter than its diff:
```python
import functools

import jax
import jax.numpy as jnp
from jax import lax
from jax.experimental import pallas as pl
from jax.experimental.pallas import tpu as pltpu
from jax.sharding import PartitionSpec as P

HDIM = 64
QLEN = 64
RUN = 16
LANES = 128
NORM_EPS = 1e-06
MASKED = -1e30
HIGHEST = lax.Precision.HIGHEST
F32 = jnp.float32
BF16 = jnp.bfloat16
VMEM_BYTES = 56 * 1024 * 1024
GELU_A = 0.7978845608028654
GELU_B = 0.044715 * GELU_A
SWAP = [(0, 0), (1, 2), (2, 1), (3, 3)]


def dot(a, b, ca, cb):
    return lax.dot_general(a, b, (((ca,), (cb,)), ((), ())), preferred_element_type=F32)


def params(grid_dims=1):
    return pltpu.CompilerParams(
        vmem_limit_bytes=VMEM_BYTES, dimension_semantics=("arbitrary",) * grid_dims
    )


def cost(flops, nbytes, trans=0):
    return pl.CostEstimate(flops=int(flops), bytes_accessed=int(nbytes), transcendentals=int(trans))


def head_stack(block):
    lane = lax.broadcasted_iota(jnp.int32, block.shape, 1)
    zero = jnp.zeros_like(block)
    return jnp.concatenate(
        [jnp.where(lane < HDIM, block, zero), jnp.where(lane < HDIM, zero, block)], axis=0
    )


def head_merge(stacked):
    lane = lax.broadcasted_iota(jnp.int32, (QLEN, LANES), 1)
    return jnp.where(lane < HDIM, stacked[:QLEN], stacked[QLEN:])


def pair_views(own_ref, oth_ref, found_ref, question, pair, local_hd, width):
    ref = own_ref if pair * LANES < local_hd else oth_ref
    base = pair * LANES % local_hd
    rows = slice(question * QLEN, (question + 1) * QLEN)
    query = ref[rows, base : base + LANES]
    key = ref[rows, local_hd + base : local_hd + base + LANES]
    value = ref[rows, 2 * local_hd + base : 2 * local_hd + base + LANES]
    col = pair * LANES
    pref = [found_ref[question, :, c * width + col : c * width + col + LANES] for c in range(4)]
    keys = jnp.concatenate([key, pref[0], pref[1]], axis=0)
    values = jnp.concatenate([value, pref[2], pref[3]], axis=0)
    stack = head_stack(query * jnp.asarray(HDIM**-0.5, BF16))
    return stack, keys, values


def pair_probs(stack, keys, bias):
    logits = dot(keys, stack, 1, 1)
    logits = jnp.concatenate([logits[:QLEN], logits[QLEN:] + bias], axis=0)
    weights = jnp.exp(logits - jnp.max(logits, axis=0, keepdims=True))
    return weights * (1.0 / jnp.sum(weights, axis=0, keepdims=True))


def attention_kernel(own_ref, oth_ref, found_ref, bias_ref, mixed_ref, *, questions, local_hd, width):
    for question in range(questions):
        bias = bias_ref[question]
        for pair in range(width // LANES):
            stack, keys, values = pair_views(
                own_ref, oth_ref, found_ref, question, pair, local_hd, width
            )
            probs = pair_probs(stack, keys, bias).astype(BF16)
            mixed = head_merge(dot(probs, values, 0, 0)).astype(BF16)
            mixed_ref[question * QLEN : (question + 1) * QLEN, pair * LANES : (pair + 1) * LANES] = mixed


def attention(own, oth, found, bias, questions=2):
    rows, local_hd = own.shape[0], own.shape[1] // 3
    width = 2 * local_hd
    count = rows // QLEN
    slots = found.shape[1]
    block = questions * QLEN
    return pl.pallas_call(
        functools.partial(attention_kernel, questions=questions, local_hd=local_hd, width=width),
        grid=(count // questions,),
        in_specs=[
            pl.BlockSpec((block, 3 * local_hd), lambda i: (i, 0)),
            pl.BlockSpec((block, 3 * local_hd), lambda i: (i, 0)),
            pl.BlockSpec((questions, slots, 4 * width), lambda i: (i, 0, 0)),
            pl.BlockSpec((questions, 2 * slots, LANES), lambda i: (i, 0, 0)),
        ],
        out_specs=pl.BlockSpec((block, width), lambda i: (i, 0)),
        out_shape=jax.ShapeDtypeStruct((rows, width), BF16),
        compiler_params=params(),
        cost_estimate=cost(rows * width * 96 * 8, rows * width * 8, rows * 12 * 96),
        name="attend",
    )(own, oth, found, bias)


def attention_back_kernel(
    own_ref, oth_ref, found_ref, bias_ref, mixed_ref, down_ref, doth_ref, slot_ref, *, questions, local_hd, width
):
    for question in range(questions):
        bias = bias_ref[question]
        rows = slice(question * QLEN, (question + 1) * QLEN)
        total = None
        for pair in range(width // LANES):
            stack, keys, values = pair_views(
                own_ref, oth_ref, found_ref, question, pair, local_hd, width
            )
            probs = pair_probs(stack, keys, bias)
            grad_stack = head_stack(mixed_ref[rows, pair * LANES : (pair + 1) * LANES])
            prob_grad = dot(values, grad_stack, 1, 1)
            delta = jnp.sum(probs * prob_grad, axis=0, keepdims=True)
            logit_grad = probs * (prob_grad - delta)
            pref_part = logit_grad[QLEN:]
            total = pref_part if total is None else total + pref_part
            low = logit_grad.astype(BF16)
            scale = HDIM**-0.5
            query_grad = head_merge(dot(low, keys, 0, 0)) * scale
            key_grad = dot(low[:QLEN], stack, 1, 0)
            value_grad = dot(probs[:QLEN].astype(BF16), grad_stack, 1, 0)
            out = down_ref if pair * LANES < local_hd else doth_ref
            base = pair * LANES % local_hd
            out[rows, base : base + LANES] = query_grad.astype(BF16)
            out[rows, local_hd + base : local_hd + base + LANES] = key_grad.astype(BF16)
            out[rows, 2 * local_hd + base : 2 * local_hd + base + LANES] = value_grad.astype(BF16)
        slot_ref[question] = jnp.broadcast_to(jnp.sum(total, axis=1, keepdims=True), total.shape)


def attention_back(own, oth, found, bias, mixed_low, questions=2):
    rows, local_hd = own.shape[0], own.shape[1] // 3
    width = 2 * local_hd
    count = rows // QLEN
    slots = found.shape[1]
    block = questions * QLEN
    wide = pl.BlockSpec((block, 3 * local_hd), lambda i: (i, 0))
    bias_spec = pl.BlockSpec((questions, 2 * slots, LANES), lambda i: (i, 0, 0))
    return pl.pallas_call(
        functools.partial(
            attention_back_kernel, questions=questions, local_hd=local_hd, width=width
        ),
        grid=(count // questions,),
        in_specs=[
            wide,
            wide,
            pl.BlockSpec((questions, slots, 4 * width), lambda i: (i, 0, 0)),
            bias_spec,
            pl.BlockSpec((block, width), lambda i: (i, 0)),
        ],
        out_specs=[wide, wide, bias_spec],
        out_shape=[
            jax.ShapeDtypeStruct((rows, 3 * local_hd), BF16),
            jax.ShapeDtypeStruct((rows, 3 * local_hd), BF16),
            jax.ShapeDtypeStruct((count, 2 * slots, LANES), F32),
        ],
        compiler_params=params(),
        cost_estimate=cost(rows * width * 96 * 20, rows * width * 16, rows * 12 * 96),
        name="attend_back",
    )(own, oth, found, bias, mixed_low)


def rms_scale(block):
    return lax.rsqrt(jnp.mean(block * block, axis=-1, keepdims=True) + NORM_EPS)


def forward_kernel(
    x_ref, mixed_ref, out_own, out_oth, gain_ref, up_own, up_oth,
    resid_ref, normed_ref, hid_own, hid_oth, slope_own, slope_oth, presid_ref, phid_own, phid_oth, *, chunk
):
    rows = x_ref.shape[0]
    half = mixed_ref.shape[1] // 2
    residual = (
        x_ref[...].astype(F32)
        + dot(mixed_ref[:, :half], out_own[...], 1, 1)
        + dot(mixed_ref[:, half:], out_oth[...], 1, 1)
    )
    resid_ref[...] = residual
    presid_ref[...] = jnp.sum(residual.reshape(rows // RUN, RUN, residual.shape[1]), axis=1)
    normed = (residual * rms_scale(residual) * gain_ref[1:2]).astype(BF16)
    normed_ref[...] = normed
    run_of = lax.broadcasted_iota(jnp.int32, (rows // RUN, rows), 0)
    row_at = lax.broadcasted_iota(jnp.int32, (rows // RUN, rows), 1)
    low = run_of * RUN
    pool = jnp.where((row_at >= low) & (row_at < low + RUN), 1.0, 0.0).astype(BF16)
    for up_ref, hid_ref, slope_ref, phid_ref in (
        (up_own, hid_own, slope_own, phid_own),
        (up_oth, hid_oth, slope_oth, phid_oth),
    ):
        for at in range(0, up_ref.shape[1], chunk):
            cols = slice(at, at + chunk)
            pre = dot(normed, up_ref[:, cols], 1, 0)
            square = pre * pre
            cube = GELU_B * square
            bend = jnp.tanh(pre * (GELU_A + cube))
            half_pre = 0.5 * pre
            hidden = (half_pre * bend + half_pre).astype(BF16)
            hid_ref[:, cols] = hidden
            slope = (0.5 + 0.5 * bend) + half_pre * (1.0 - bend * bend) * (GELU_A + 3.0 * cube)
            slope_ref[:, cols] = slope.astype(BF16)
            phid_ref[:, cols] = dot(pool, hidden, 1, 0)


def forward(x, mixed, out_pair, gains, up_pair, tile=256, chunk=512):
    rows, width = x.shape
    local_ff = up_pair[0].shape[1]
    row = lambda cols: pl.BlockSpec((tile, cols), lambda i: (i, 0))
    pooled = lambda cols: pl.BlockSpec((tile // RUN, cols), lambda i: (i, 0))
    whole = lambda a: pl.BlockSpec(a.shape, lambda i: (0, 0))
    shape = jax.ShapeDtypeStruct
    return pl.pallas_call(
        functools.partial(forward_kernel, chunk=chunk),
        grid=(rows // tile,),
        in_specs=[row(width), row(width), whole(out_pair[0]), whole(out_pair[1]), whole(gains), whole(up_pair[0]), whole(up_pair[1])],
        out_specs=[row(width), row(width)] + [row(local_ff)] * 4 + [pooled(width), pooled(local_ff), pooled(local_ff)],
        out_shape=[
            shape((rows, width), F32),
            shape((rows, width), BF16),
            shape((rows, local_ff), BF16),
            shape((rows, local_ff), BF16),
            shape((rows, local_ff), BF16),
            shape((rows, local_ff), BF16),
            shape((rows // RUN, width), F32),
            shape((rows // RUN, local_ff), F32),
            shape((rows // RUN, local_ff), F32),
        ],
        compiler_params=params(),
        cost_estimate=cost(2 * rows * width * (width + 2 * local_ff), rows * (width * 9 + local_ff * 8) + width * (width + local_ff * 2) * 2, rows * local_ff * 2),
        name="out_up",
    )(x, mixed, *out_pair, gains, *up_pair)


def norm_back(block, grad, gain):
    scale = rms_scale(block)
    weighted = grad * gain
    inner = jnp.mean(block * weighted, axis=-1, keepdims=True)
    return (
        scale * weighted - block * (scale * scale * scale * inner),
        jnp.sum(grad * block * scale, axis=0, keepdims=True),
    )


def backward_kernel(
    cot_ref, spread_ref, resid_ref, slope_own, slope_oth, down_own, down_oth, up_own, up_oth, gain_ref, out_own, out_oth,
    result_ref, pre_own, pre_oth, rgrad_ref, attn_ref, mixed_ref, gain_grad_ref, *, chunk
):
    rows, width = cot_ref.shape
    spread = jnp.broadcast_to(spread_ref[...][:, None, :], (rows // RUN, RUN, width)).reshape(rows, width)
    result_grad = cot_ref[...].astype(F32) + spread
    result_low = result_grad.astype(BF16)
    result_ref[...] = result_low
    total = jnp.zeros((rows, width), F32)
    for down_ref, up_ref, slope_ref, pre_ref in (
        (down_own, up_own, slope_own, pre_own),
        (down_oth, up_oth, slope_oth, pre_oth),
    ):
        for at in range(0, up_ref.shape[1], chunk):
            cols = slice(at, at + chunk)
            hidden_grad = dot(result_low, down_ref[:, cols], 1, 0)
            pre_low = (hidden_grad * slope_ref[:, cols].astype(F32)).astype(BF16)
            pre_ref[:, cols] = pre_low
            total = total + dot(pre_low, up_ref[:, cols], 1, 1)
    part, gain_part = norm_back(resid_ref[...], total, gain_ref[1:2])
    residual_grad = result_grad + part
    rgrad_ref[...] = residual_grad
    attn_low = residual_grad.astype(BF16)
    attn_ref[...] = attn_low
    half = out_own.shape[1]
    mixed_ref[:, :half] = dot(attn_low, out_own[...], 1, 0).astype(BF16)
    mixed_ref[:, half:] = dot(attn_low, out_oth[...], 1, 0).astype(BF16)

    @pl.when(pl.program_id(0) == 0)
    def _():
        gain_grad_ref[...] = jnp.zeros_like(gain_grad_ref)

    gain_grad_ref[...] += jnp.broadcast_to(gain_part, gain_grad_ref.shape)


def backward(cot, spread, residual, slopes, down_pair, up_pair, gains, out_pair, tile=256, chunk=512):
    rows, width = cot.shape
    local_ff = up_pair[0].shape[1]
    row = lambda cols: pl.BlockSpec((tile, cols), lambda i: (i, 0))
    whole = lambda a: pl.BlockSpec(a.shape, lambda i: (0, 0))
    shape = jax.ShapeDtypeStruct
    return pl.pallas_call(
        functools.partial(backward_kernel, chunk=chunk),
        grid=(rows // tile,),
        in_specs=[
            row(width),
            pl.BlockSpec((tile // RUN, width), lambda i: (i, 0)),
            row(width),
            row(local_ff),
            row(local_ff),
            whole(down_pair[0]),
            whole(down_pair[1]),
            whole(up_pair[0]),
            whole(up_pair[1]),
            whole(gains),
            whole(out_pair[0]),
            whole(out_pair[1]),
        ],
        out_specs=[row(width), row(local_ff), row(local_ff), row(width), row(width), row(width), pl.BlockSpec((8, width), lambda i: (0, 0))],
        out_shape=[
            shape((rows, width), BF16),
            shape((rows, local_ff), BF16),
            shape((rows, local_ff), BF16),
            shape((rows, width), F32),
            shape((rows, width), BF16),
            shape((rows, width), BF16),
            shape((8, width), F32),
        ],
        compiler_params=params(),
        cost_estimate=cost(2 * rows * width * (width + 4 * local_ff), rows * (width * 16 + local_ff * 8) + width * (width + local_ff * 4) * 2),
        name="down_up_back",
    )(cot, spread, residual, *slopes, *down_pair, *up_pair, gains, *out_pair)


def input_kernel(x_ref, rgrad_ref, d_own, d_oth, w_own, w_oth, gain_ref, out_ref, gain_grad_ref):
    normed_grad = dot(d_own[...], w_own[...], 1, 1) + dot(d_oth[...], w_oth[...], 1, 1)
    part, gain_part = norm_back(x_ref[...].astype(F32), normed_grad, gain_ref[0:1])
    out_ref[...] = (rgrad_ref[...] + part).astype(BF16)

    @pl.when(pl.program_id(0) == 0)
    def _():
        gain_grad_ref[...] = jnp.zeros_like(gain_grad_ref)

    gain_grad_ref[...] += jnp.broadcast_to(gain_part, gain_grad_ref.shape)


def input_back(x, rgrad, d_pair, w_pair, gains, tile=256):
    rows, width = x.shape
    row = lambda cols: pl.BlockSpec((tile, cols), lambda i: (i, 0))
    whole = lambda a: pl.BlockSpec(a.shape, lambda i: (0, 0))
    wide = d_pair[0].shape[1]
    return pl.pallas_call(
        input_kernel,
        grid=(rows // tile,),
        in_specs=[row(width), row(width), row(wide), row(wide), whole(w_pair[0]), whole(w_pair[1]), whole(gains)],
        out_specs=[row(width), pl.BlockSpec((8, width), lambda i: (0, 0))],
        out_shape=[jax.ShapeDtypeStruct((rows, width), BF16), jax.ShapeDtypeStruct((8, width), F32)],
        compiler_params=params(),
        cost_estimate=cost(4 * rows * width * wide, rows * (width * 8 + wide * 4) + width * wide * 4),
        name="qkv_back",
    )(x, rgrad, *d_pair, *w_pair, gains)


def swapped(value):
    return lax.ppermute(value, ("half", "mp"), SWAP)


def from_mate(value):
    return lax.ppermute(value, "half", [(0, 1), (1, 0)])


def pick(value, index, axis=0):
    return lax.dynamic_index_in_dim(value, index, axis, keepdims=False)


def fetch(weight):
    own = swapped(weight)
    return own, from_mate(own)


def scatter_sum(own, oth):
    grad = (own.astype(F32) + from_mate(oth).astype(F32)).astype(BF16)
    shards = lax.axis_size("dp")
    if shards != 8:
        return lax.psum_scatter(grad.astype(F32), "dp", scatter_dimension=0, tiled=True)
    rows, cols = grad.shape
    index = lax.axis_index("dp")
    x_at, z_at = index % 2, index // 2
    view = grad.reshape(4, 2, rows // 8, cols)
    got = lax.ppermute(pick(view, 1 - x_at, 1), "dp", [(i, i ^ 1) for i in range(8)])
    part = (pick(view, x_at, 1).astype(F32) + got.astype(F32)).astype(BF16)
    up = down = None
    for step in range(1, 4):
        val = pick(part, jnp.minimum(z_at + 4 - step, 3))
        if up is not None:
            val = (val.astype(F32) + up.astype(F32)).astype(BF16)
        up = lax.ppermute(val, "dp", [(2 * z + x, 2 * z + 2 + x) for z in range(step) for x in range(2)])
        val = pick(part, jnp.maximum(z_at - 4 + step, 0))
        if down is not None:
            val = (val.astype(F32) + down.astype(F32)).astype(BF16)
        down = lax.ppermute(val, "dp", [(2 * z + x, 2 * z - 2 + x) for z in range(4 - step, 4) for x in range(2)])
    return pick(part, z_at).astype(F32) + up.astype(F32) + down.astype(F32)


def all_sum(value):
    return lax.psum(value, ("half", "dp"))


def body(tokens, norm_gains, qkv_w, out_w, up_w, down_w, memory, memory_ids, counts, prefix_mask, cotangent):
    core = lax.axis_index("half")
    layer = lax.axis_index("mp")
    shard_count = lax.axis_size("dp")
    shard_index = lax.axis_index("dp")
    rows, width = tokens.shape[1:]
    questions, k_most = memory_ids.shape
    mem_dev = memory.shape[1]
    score_scale = (4 * width) ** (-0.5)
    local_hd = qkv_w.shape[3]
    padded = 16

    qkv_pair = fetch(qkv_w[0].reshape(width, 3 * local_hd))
    x = swapped(tokens[0])
    gains = swapped(norm_gains[0])
    out_pair = fetch(out_w[0])
    up_pair = fetch(up_w[0])
    down_pair = fetch(down_w[0])
    cot = swapped(cotangent[0])

    slot_total = questions * k_most
    capacity = (slot_total + shard_count - 1) // shard_count
    table = memory[0].reshape(mem_dev, 4 * width)
    local_rows = jnp.concatenate(
        [memory_ids.reshape(-1) % mem_dev, jnp.zeros((capacity * shard_count - slot_total,), jnp.int32)]
    )
    requests = jnp.roll(local_rows.reshape(capacity, shard_count), shard_index, axis=1).T
    asked = lax.all_to_all(requests, "dp", split_axis=0, concat_axis=0, tiled=True).reshape(-1)
    answer = dot((asked[:, None] == jnp.arange(mem_dev)[None, :]).astype(BF16), table, 1, 0).astype(BF16)
    answers = lax.all_to_all(answer, "dp", split_axis=0, concat_axis=0, tiled=True)
    answers = swapped(answers)
    at = jnp.arange(questions * padded)
    slot = at % padded
    flat = at // padded * k_most + slot
    source = (shard_index + flat % shard_count) % shard_count * capacity + flat // shard_count
    source = jnp.where(slot < k_most, source, -1)
    chosen = (source[:, None] == jnp.arange(capacity * shard_count)[None, :]).astype(BF16)
    found = dot(chosen, answers, 1, 0).astype(BF16).reshape(questions, padded, 4 * width)
    halves = found.reshape(questions, padded, 4, 2, width // 2)
    found_heads = jnp.where(core == 0, found, halves[:, :, :, ::-1].reshape(found.shape))

    valid = (jnp.arange(k_most)[None, :] < counts[:, None])[:, None, :] & (
        jnp.swapaxes(prefix_mask.reshape(questions, k_most, 2), 1, 2) == 1
    )
    valid = jnp.pad(valid.astype(F32), ((0, 0), (0, 0), (0, padded - k_most))).reshape(questions, 2 * padded)
    valid = (swapped(valid) > 0.5) & (layer == 1)

    def biases(scores):
        wide = jnp.tile(jnp.pad(scores.astype(F32), ((0, 0), (0, padded - k_most))), (1, 2))
        bias = jnp.where(valid, wide, MASKED)
        return jnp.broadcast_to(bias[:, :, None], (questions, 2 * padded, LANES))

    x32 = x.astype(F32)
    normed = (x32 * rms_scale(x32) * gains[0]).astype(BF16)
    proj = tuple(dot(normed, w, 1, 0).astype(BF16) for w in qkv_pair)

    def layer_forward(scores):
        bias = biases(scores)
        mixed = attention(*proj, found_heads, bias)
        return bias, mixed, forward(x, mixed, out_pair, gains, up_pair)

    first = layer_forward(jnp.zeros((questions, k_most), BF16))[2]
    pooled = first[6] + sum(
        lax.dot_general(p, w.astype(F32), (((1,), (1,)), ((), ())), precision=HIGHEST, preferred_element_type=F32)
        for p, w in zip(first[7:9], down_pair)
    )
    pooled = (pooled * (1.0 / RUN)).reshape(questions, 4 * width)
    scores = jnp.sum(pooled[:, None, :] * found[:, :k_most].astype(F32), axis=-1) * score_scale
    sent = lax.ppermute(scores.astype(BF16), "mp", [(0, 1)])

    bias, mixed, (residual, normed_two, hid_own, hid_oth, slope_own, slope_oth, _, _, _) = layer_forward(sent)

    def layer_backward(spread):
        result_low, pre_own, pre_oth, rgrad, attn_low, mixed_low, gain_two = backward(
            cot, spread, residual, (slope_own, slope_oth), down_pair, up_pair, gains, out_pair
        )
        d_own, d_oth, slot_grad = attention_back(*proj, found_heads, bias, mixed_low)
        return result_low, (pre_own, pre_oth), rgrad, attn_low, gain_two, (d_own, d_oth), slot_grad

    slot_grad = layer_backward(jnp.zeros((rows // RUN, width), F32))[-1][:, :, 0]
    score_low = (slot_grad[:, :k_most] + slot_grad[:, padded : padded + k_most]).astype(BF16)
    score_in = lax.ppermute(score_low, "mp", [(1, 0)])
    scale = score_scale / RUN
    spread = jnp.sum(
        (score_in.astype(F32) * scale)[:, :, None] * found[:, :k_most].astype(F32), axis=1
    ).reshape(rows // RUN, width)
    result_low, pre_pair, rgrad, attn_low, gain_two, d_pair, _ = layer_backward(spread)
    grad_in, gain_one = input_back(x, rgrad, d_pair, qkv_pair, gains)

    result = residual + dot(hid_own, down_pair[0], 1, 1) + dot(hid_oth, down_pair[1], 1, 1)
    activations = swapped(result.astype(BF16))
    input_grad = swapped(grad_in).astype(F32)
    score_out = swapped(jnp.where(layer == 1, score_low, score_in)).astype(F32)
    gain_grads = swapped(all_sum(jnp.concatenate([gain_one[:1], gain_two[:1]], axis=0)))

    def weight_grad(rows_of, cols_of):
        return dot(rows_of, cols_of, 0, 0).astype(BF16)

    local_mixed = (mixed[:, :local_hd], mixed[:, local_hd:])
    down_g = swapped(scatter_sum(weight_grad(result_low, hid_own), weight_grad(result_low, hid_oth)))
    up_g = swapped(scatter_sum(*(weight_grad(normed_two, p) for p in pre_pair)))
    out_g = swapped(scatter_sum(*(weight_grad(attn_low, m) for m in local_mixed)))
    qkv_g = swapped(scatter_sum(*(weight_grad(normed, d) for d in d_pair)))
    return (
        activations[None],
        input_grad[None],
        score_out,
        gain_grads[None],
        qkv_g.reshape(1, -1, 3, local_hd),
        out_g[None],
        up_g[None],
        down_g[None],
    )


def solution(mesh):
    placed = (
        P("half", ("dp", "mp"), None),
        P("half", None, None),
        P("half", None, None, "mp"),
        P("half", None, "mp"),
        P("half", None, "mp"),
        P("half", None, "mp"),
        P("half", "dp", None, None),
        P(("dp", "mp"), None),
        P(("dp", "mp")),
        P(("dp", "mp"), None),
        P("half", ("dp", "mp"), None),
    )
    return jax.shard_map(
        body,
        mesh=mesh,
        in_specs=placed,
        out_specs=(
            P("half", ("dp", "mp"), None),
            P("half", ("dp", "mp"), None),
            P(("dp", "mp"), None),
            P("half", None, None),
            P("half", "dp", None, "mp"),
            P("half", "dp", "mp"),
            P("half", "dp", "mp"),
            P("half", "dp", "mp"),
        ),
        check_vma=False,
    )
```

time: 1500 us -> 686 us (0.46)
  local copies, waits for them, and re-layouts: 383 us -> 41.5 us
  blocking collectives: 297 us -> 28.6 us
  matrix products: 279 us -> 61.9 us
  Pallas kernels: 0 us -> 213 us
  waiting for transfers between devices: 347 us -> 163 us
  starting transfers between devices: 43.3 us -> 146 us
  other arithmetic: 112 us -> 17.1 us
  between operations: 19.6 us -> 2.21 us
    reduce_scatter x24 -> x0, waiting for transfers between devices: 328 us -> none  [the longest x1 99.3 us: reduce_grads(): lax.psum_scatter(matrices[2], 'dp', scatter_dimension=0, tiled=True)]
    all_gather x25 -> x0, blocking collectives: 250 us -> none  [the longest x10 116 us: grad_rows(): return lax.all_gather(grad_low, 'mp', axis=0, tiled=True)]
    dot_general x129 -> x16, matrix products: 279 us -> 61.9 us  [the longest x14 53.9 us: dot(): lax.dot_general(a, b, (((ca,), (cb,)), ((), ())), preferred_element_type=...]
    pallas_call x0 -> x9, Pallas kernels: none -> 213 us  [the longest x2 56.4 us: attention(): pl.pallas_call(functools.partial(attention_kernel, questions=questions, l...]
    ppermute x8 -> x55, waiting for transfers between devices: 11.8 us -> 162 us  [the longest x17 70.9 us: swapped(): return lax.ppermute(value, ('half', 'mp'), SWAP)]
    another operation x71 -> x6, local copies, waits for them, and re-layouts: 140 us -> 3.57 us  [the longest x1 2.21 us: body(): qkv_pair = fetch(qkv_w[0].reshape(width, 3 * local_hd))]
    ppermute x8 -> x55, starting transfers between devices: 24.1 us -> 135 us  [the longest x17 63.7 us: swapped(): return lax.ppermute(value, ('half', 'mp'), SWAP)]
    dynamic_slice x40 -> x0, local copies, waits for them, and re-layouts: 65.9 us -> none  [the longest x39 65.5 us: select_block(): return lax.dynamic_index_in_dim(stack_arr, block_index, 0, keepdims=False)]
  transfers between devices with their start and end apart: 35 -> 57, of which waited for: 16 -> 19; matrix products, arithmetic and copies ran while one was open for 31% -> 16% of each run, Pallas kernels for 0% -> 24%
where the time goes in v1:
time: 686 us; the launch traced here: 674 us
  Pallas kernels  213 us (31%)
  waiting for transfers between devices  163 us (24%)
  starting transfers between devices  146 us (21%)
  matrix products  61.9 us (9%)
  local copies, waits for them, and re-layouts  41.5 us (6%)
  blocking collectives  28.6 us (4%)
  other arithmetic  17.1 us (2%)
    ppermute x17, waiting for transfers between devices, swapped(): return lax.ppermute(value, ('half', 'mp'), SWAP)  70.9 us
    ppermute x17, starting transfers between devices, swapped(): return lax.ppermute(value, ('half', 'mp'), SWAP)  63.7 us
    ppermute x4, waiting for transfers between devices, scatter_sum(): lax.ppermute(pick(view, 1 - x_at, 1), 'dp', [(i, i ^ 1) for i in range(8)])  56.6 us
    pallas_call x2, Pallas kernels, attention(): pl.pallas_call(functools.partial(attention_kernel, questions=questions, l...  56.4 us
    pallas_call x2, Pallas kernels, attention_back(): pl.pallas_call(functools.partial(attention_back_kernel, questions=questio...  54.9 us
    dot_general x14, matrix products, dot(): lax.dot_general(a, b, (((ca,), (cb,)), ((), ())), preferred_element_type=...  53.9 us
    pallas_call x2, Pallas kernels, forward(): pl.pallas_call(functools.partial(forward_kernel, chunk=chunk), grid=(rows...  46.5 us
    pallas_call x2, Pallas kernels, backward(): pl.pallas_call(functools.partial(backward_kernel, chunk=chunk), grid=(row...  45.4 us
  transfers between devices with their start and end apart: 57, of which 19 were waited for; matrix products, arithmetic and copies ran while one was open for 16% of the time, Pallas kernels for 24%

profile of v1, /device:TPU:17, one launch (start us, length us, event | category | flops | bytes accessed | tf_op | source)
XLA Modules:
  0.0 673.8 jit_solution(6046636762463350145)
XLA Ops:
  5.9 5.6 all-to-all-start
  19.7 5.6 all-to-all-start.1
  42.1 50.2 %collective-permute-done.5 = f32[16,32]{1,0:T(8,128)S(1)} collective-permute-done((f32[16,32]{1,0:T(8,128)S(1)}, f32[16,32]{1,0:T(8,128)S(1)}, u32[]{:S(2)}, u32[]{:S(2)}) %collective-permute-start.5) | collective-permute-done | bytes 2080 | tf_op jit(solution)/shard_map/ppermute | solution.py:357
  105.3 5.7 convolution_convert_fusion.2.own_ref
  111.0 8.0 %collective-permute-done.6.out_own = bf16[768,384]{1,0:T(8,128)(2,1)} collective-permute-done((bf16[768,384]{1,0:T(8,128)(2,1)S(1)}, bf16[768,384]{1,0:T(8,128)(2,1)}, u32[]{:S(2)}, u32[]{:S(2)}) %collective-permute-start.6) | collective-permute-done | bytes 589856 | tf_op jit(solution)/shard_map/ppermute | solution.py:357
  126.4 11.3 %rev.3 = bf16[16,16,4,2,384]{4,3,2,1,0:T(2,128)(2,1)} reverse(bf16[16,16,4,2,384]{4,3,2,1,0:T(2,128)(2,1)S(1)} %reshape_reshape.3), dimensions={3} | reverse | bytes 3145728 | tf_op jit(solution)/shard_map/rev | solution.py:440
  142.9 5.7 convolution_convert_fusion.1.oth_ref
  149.5 28.0 %attend.2.mixed_ref = bf16[1024,768]{1,0:T(8,128)(2,1)} custom-call(bf16[1024,1152]{1,0:T(8,128)(2,1)} %convolution_convert_fusion.2.own_ref, bf16[1024,1152]{1,0:T(8,128)(2,1)} %convolution_convert_fusion.1.oth_ref, bf16[16,16,3072]{2,1,0:T(8,128)(2,1)} %broadcast_select_fusion.found_ref, f32[16,32,128]{2,1,0:T(8,128)} %broadcast_in_dim.52.bias_ref), custom_call_target="tpu_custom_call" | custom-call | flops 603979776 | bytes 6291456 | tf_op jit(solution)/shard_map/attend/pallas_call | solution.py:92
  177.5 23.3 %out_up.2 = (f32[1024,768]{1,0:T(8,128)}, bf16[1024,768]{1,0:T(8,128)(2,1)}, bf16[1024,1536]{1,0:T(8,128)(2,1)}, bf16[1024,1536]{1,0:T(8,128)(2,1)}, bf16[1024,1...) custom-call(bf16[1024,768]{1,0:T(8,128)(2,1)} %collective-permute-do, ...), custom_call_target="tpu_custom_call" | custom-call | flops 6039797760 | bytes 25559040 | tf_op jit(solution)/shard_map/out_up/pallas_call | solution.py:220
  214.8 28.4 %attend.3.mixed_ref = bf16[1024,768]{1,0:T(8,128)(2,1)} custom-call(bf16[1024,1152]{1,0:T(8,128)(2,1)} %convolution_convert_fusion.2.own_ref, bf16[1024,1152]{1,0:T(8,128)(2,1)} %convolution_convert_fusion.1.oth_ref, bf16[16,16,3072]{2,1,0:T(8,128)(2,1)} %broadcast_select_fusion.found_ref, f32[16,32,128]{2,1,0:T(8,128)} %broadcast_in_dim.53.bias_ref), custom_call_target="tpu_custom_call" | custom-call | flops 603979776 | bytes 6291456 | tf_op jit(solution)/shard_map/attend/pallas_call | solution.py:92
  243.2 23.3 %out_up.3 = (f32[1024,768]{1,0:T(8,128)}, bf16[1024,768]{1,0:T(8,128)(2,1)}, bf16[1024,1536]{1,0:T(8,128)(2,1)}, bf16[1024,1536]{1,0:T(8,128)(2,1)}, bf16[1024,1...) custom-call(bf16[1024,768]{1,0:T(8,128)(2,1)} %collective-permute-do, ...), custom_call_target="tpu_custom_call" | custom-call | flops 6039797760 | bytes 25559040 | tf_op jit(solution)/shard_map/out_up/pallas_call | solution.py:220
  267.1 22.7 %down_up_back.2 = (bf16[1024,768]{1,0:T(8,128)(2,1)}, bf16[1024,1536]{1,0:T(8,128)(2,1)}, bf16[1024,1536]{1,0:T(8,128)(2,1)}, f32[1024,768]{1,0:T(8,128)}, bf16[...) custom-call(bf16[1024,768]{1,0:T(8,128)(2,1)} %collective-permute-done.14.cot_ref, ...), custom_call_target="tpu_custom_call" | custom-call | flops 10871635968 | bytes 35782656 | tf_op jit(solution)/shard_map/down_up_back/pallas_call | solution.py:294
  289.9 27.5 %attend_back.2 = (bf16[1024,1152]{1,0:T(8,128)(2,1)}, bf16[1024,1152]{1,0:T(8,128)(2,1)}, f32[16,32,128]{2,1,0:T(8,128)}) custom-call(bf16[1024,1152]{1,0:T(8,128)(2,1)} %convolution_convert_fusion.2.own_ref, bf16[1024,1152]{1,0:T(8,128)(2,1)} %convolution_convert_fusion.1.oth_ref, bf16[16,16,3072]{2,1,0:T(8,128)(2,1)} %broadcast_select_fusion.found_ref, ...), custom_call_target="tpu_custom_call" | custom-call | flops 1509949440 | bytes 12582912 | tf_op jit(solution)/shard_map/attend_back/pallas_call | solution.py:148
  324.4 5.4 add_convert_fusion.3
  329.8 5.2 collective-permute-start.13
  336.6 22.7 %down_up_back.3 = (bf16[1024,768]{1,0:T(8,128)(2,1)}, bf16[1024,1536]{1,0:T(8,128)(2,1)}, bf16[1024,1536]{1,0:T(8,128)(2,1)}, f32[1024,768]{1,0:T(8,128)}, bf16[...) custom-call(bf16[1024,768]{1,0:T(8,128)(2,1)} %collective-permute-done.14.cot_ref, ...), custom_call_target="tpu_custom_call" | custom-call | flops 10871635968 | bytes 35782656 | tf_op jit(solution)/shard_map/down_up_back/pallas_call | solution.py:294
  359.3 5.2 convolution_convert_fusion.5
  368.6 9.1 %collective-permute-start.46 = (bf16[768,1536]{1,0:T(8,128)(2,1)}, bf16[768,1536]{1,0:T(8,128)(2,1)}, u32[]{:S(2)}, u32[]{:S(2)}) collective-permute-start(bf16[768,1536]{1,0:T(8,128)(2,1)} %convolution_convert_fusion.4), channel_id=1, source_target_pairs={{0,16},{16,0},{1,17},{17,1},{2,18},{18,2},{3,19},{19,3},{4,20},{20... | collective-permute-start | bytes 7077896 | tf_op jit(solution)/shard_map/ppermute | solution.py:361
  378.7 27.4 %attend_back.3 = (bf16[1024,1152]{1,0:T(8,128)(2,1)}, bf16[1024,1152]{1,0:T(8,128)(2,1)}, f32[16,32,128]{2,1,0:T(8,128)}) custom-call(bf16[1024,1152]{1,0:T(8,128)(2,1)} %convolution_convert_fusion.2.own_ref, bf16[1024,1152]{1,0:T(8,128)(2,1)} %convolution_convert_fusion.1.oth_ref, bf16[16,16,3072]{2,1,0:T(8,128)(2,1)} %broadcast_select_fusion.found_ref, ...), custom_call_target="tpu_custom_call" | custom-call | flops 1509949440 | bytes 12582912 | tf_op jit(solution)/shard_map/attend_back/pallas_call | solution.py:148
  406.1 5.9 convolution_convert_fusion.8
  423.0 5.0 convolution_convert_fusion.9
  431.2 9.7 %qkv_back.1 = (bf16[1024,768]{1,0:T(8,128)(2,1)}, f32[8,768]{1,0:T(8,128)}) custom-call(bf16[1024,768]{1,0:T(8,128)(2,1)} %collective-permute-done.x_ref, f32[1024,768]{1,0:T(8,128)} %get-tuple-element.40.rgrad_ref, bf16[1024,1152]{1,0:T(8,128)(2,1)} %get-tuple-element.42.d_own, bf16[1024,1152]{1,0:T(8,128)(2,1)} %get-tuple-element.43.d_oth, ...), custom_call_target="tpu_custom_call" | custom-call | flops 3623878656 | bytes 14548992 | tf_op jit(solution)/shard_map/qkv_back/pallas_call | solution.py:344
  450.3 28.6 %psum.7 = f32[2,768]{1,0:T(2,128)S(1)} all-reduce(f32[2,768]{1,0:T(2,128)S(1)} %pad_maximum_fusion), channel_id=1, replica_groups=mesh['half'=2,'dp'=8,'mp'=2] {'half','dp'}, use_global_device_ids=true, to_apply=%region_3.4 | all-reduce | flops 1536 | bytes 12288 | tf_op jit(solution)/shard_map/psum | solution.py:398
  481.6 5.0 collective-permute-start.35
  498.9 15.6 %collective-permute-done.20 = bf16[4,96,1152]{2,1,0:T(8,128)(2,1)S(1)} collective-permute-done((bf16[4,96,1152]{2,1,0:T(8,128)(2,1)S(1)}, bf16[4,96,1152]{2,1,0:T(8,128)(2,1)S(1)}, u32[]{:S(2)}, u32[]{:S(2)}) %collective-permute-start.20) | collective-permute-done | bytes 884768 | tf_op jit(solution)/shard_map/ppermute | solution.py:382
  520.5 6.2 collective-permute-done.24
  539.2 14.3 %collective-permute-done.47 = bf16[4,96,1536]{2,1,0:T(8,128)(2,1)S(1)} collective-permute-done((bf16[4,96,1536]{2,1,0:T(8,128)(2,1)S(1)}, bf16[4,96,1536]{2,1,0:T(8,128)(2,1)S(1)}, u32[]{:S(2)}, u32[]{:S(2)}) %collective-permute-start.47) | collective-permute-done | bytes 1179680 | tf_op jit(solution)/shard_map/ppermute | solution.py:382
  554.5 24.2 %collective-permute-done.38 = bf16[4,96,1536]{2,1,0:T(8,128)(2,1)S(1)} collective-permute-done((bf16[4,96,1536]{2,1,0:T(8,128)(2,1)S(1)}, bf16[4,96,1536]{2,1,0:T(8,128)(2,1)S(1)}, u32[]{:S(2)}, u32[]{:S(2)}) %collective-permute-start.38) | collective-permute-done | bytes 1179680 | tf_op jit(solution)/shard_map/ppermute | solution.py:382
  582.6 4.9 collective-permute-done.51
  588.8 6.3 collective-permute-done.49
  623.7 12.5 %collective-permute-start.18 = (f32[2,768]{1,0:T(2,128)S(1)}, f32[2,768]{1,0:T(2,128)S(1)}, u32[]{:S(2)}, u32[]{:S(2)}) collective-permute-start(f32[2,768]{1,0:T(2,128)S(1)} %psum.7), channel_id=1, source_target_pairs={{0,0},{1,16},{16,1},{17,17},{2,2},{3,18},{18,3},{19,19},{4,4},{5,2... | collective-permute-start | bytes 18440 | tf_op jit(solution)/shard_map/ppermute | solution.py:357
  655.4 11.6 %collective-permute-done.27 = f32[96,1152]{1,0:T(8,128)S(1)} collective-permute-done((f32[96,1152]{1,0:T(8,128)S(1)}, f32[96,1152]{1,0:T(8,128)S(1)}, u32[]{:S(2)}, u32[]{:S(2)}) %collective-permute-start.27) | collective-permute-done | bytes 442400 | tf_op jit(solution)/shard_map/ppermute | solution.py:357
  (244 shorter events, 201.4 us)
Async XLA Ops:
  0.6 102.2 %collective-permute-start.8 = (bf16[768,1536]{1,0:T(8,128)(2,1)}, bf16[768,1536]{1,0:T(8,128)(2,1)}, u32[]{:S(2)}, u32[]{:S(2)}) collective-permute-start(bf16[768,1536]{1,0:T(8,128)(2,1)} %bitcast.177), channel_id=1, source_target_pairs={{0,0},{1,16},{16,1},{17,17},{2,2},{3,18},{18,3},{19,19},{4,4},{5,2... | collective-permute-start | bytes 7077896 | tf_op jit(solution)/shard_map/ppermute | solution.py:357
  19.7 76.2 %all-to-all-start.1 = ((bf16[8,20,3072]{2,1,0:T(8,128)(2,1)}), bf16[8,20,3072]{2,1,0:T(8,128)(2,1)S(1)}, u32[]{:S(2)}, u32[]{:S(2)}) async-start(bf16[8,20,3072]{2,1,0:T(8,128)(2,1)} %all_to_all.16), calls=%async_computation.1 | async-start | bytes 2359296 | tf_op jit(solution)/shard_map/all_to_all | solution.py:430
  25.3 75.6 %collective-permute-start = (bf16[1024,768]{1,0:T(8,128)(2,1)}, bf16[1024,768]{1,0:T(8,128)(2,1)}, u32[]{:S(2)}, u32[]{:S(2)}) collective-permute-start(bf16[1024,768]{1,0:T(8,128)(2,1)} %bitcast), channel_id=1, source_target_pairs={{0,0},{1,16},{16,1},{17,17},{2,2},{3,18},{18,3},{19,19},{4,4},{5,2... | collective-permute-start | bytes 4718600 | tf_op jit(solution)/shard_map/ppermute | solution.py:357
  33.8 70.9 %collective-permute-start.2 = (bf16[768,1152]{1,0:T(8,128)(2,1)}, bf16[768,1152]{1,0:T(8,128)(2,1)}, u32[]{:S(2)}, u32[]{:S(2)}) collective-permute-start(bf16[768,1152]{1,0:T(8,128)(2,1)} %copy.54), channel_id=1, source_target_pairs={{0,0},{1,16},{16,1},{17,17},{2,2},{3,18},{18,3},{19,19},{4,4},{5,2... | collective-permute-start | bytes 5308424 | tf_op jit(solution)/shard_map/ppermute | solution.py:357
  35.9 87.0 %collective-permute-start.10 = (bf16[768,1536]{1,0:T(8,128)(2,1)}, bf16[768,1536]{1,0:T(8,128)(2,1)}, u32[]{:S(2)}, u32[]{:S(2)}) collective-permute-start(bf16[768,1536]{1,0:T(8,128)(2,1)} %bitcast.178), channel_id=1, source_target_pairs={{0,0},{1,16},{16,1},{17,17},{2,2},{3,18},{18,3},{19,19},{4,4},{5,2... | collective-permute-start | bytes 7077896 | tf_op jit(solution)/shard_map/ppermute | solution.py:357
  40.0 52.3 %collective-permute-start.5 = (f32[16,32]{1,0:T(8,128)S(1)}, f32[16,32]{1,0:T(8,128)S(1)}, u32[]{:S(2)}, u32[]{:S(2)}) collective-permute-start(f32[16,32]{1,0:T(8,128)S(1)} %reshape.220), channel_id=1, source_target_pairs={{0,0},{1,16},{16,1},{17,17},{2,2},{3,18},{18,3},{19,19},{4,4},{5,2... | collective-permute-start | bytes 6152 | tf_op jit(solution)/shard_map/ppermute | solution.py:357
  97.2 27.3 %collective-permute-start.4 = (bf16[160,3072]{1,0:T(8,128)(2,1)S(1)}, bf16[160,3072]{1,0:T(8,128)(2,1)S(1)}, u32[]{:S(2)}, u32[]{:S(2)}) collective-permute-start(bf16[160,3072]{1,0:T(8,128)(2,1)S(1)} %all_to_all.18), channel_id=1, source_target_pairs={{0,0},{1,16},{16,1},{17,17},{2,2},{3,18},{18,3},{19,19},{4,4},{5,2... | collective-permute-start | bytes 2949128 | tf_op jit(solution)/shard_map/ppermute | solution.py:357
  100.9 18.1 %collective-permute-start.6 = (bf16[768,384]{1,0:T(8,128)(2,1)S(1)}, bf16[768,384]{1,0:T(8,128)(2,1)}, u32[]{:S(2)}, u32[]{:S(2)}) collective-permute-start(bf16[768,384]{1,0:T(8,128)(2,1)S(1)} %bitcast.179), channel_id=1, source_target_pairs={{0,0},{1,16},{16,1},{17,17},{2,2},{3,18},{18,3},{19,19},{4,4},{5,2... | collective-permute-start | bytes 1769480 | tf_op jit(solution)/shard_map/ppermute | solution.py:357
  102.8 74.7 %collective-permute-start.9 = (bf16[768,1536]{1,0:T(8,128)(2,1)}, bf16[768,1536]{1,0:T(8,128)(2,1)}, u32[]{:S(2)}, u32[]{:S(2)}) collective-permute-start(bf16[768,1536]{1,0:T(8,128)(2,1)} %collective-permute-done.8.up_own), channel_id=1, source_target_pairs={{0,16},{16,0},{1,17},{17,1},{2,18},{18,2},{3,19},{19,3},{4,20},{20... | collective-permute-start | bytes 7077896 | tf_op jit(solution)/shard_map/ppermute | solution.py:361
  104.7 38.2 %collective-permute-start.3 = (bf16[768,1152]{1,0:T(8,128)(2,1)}, bf16[768,1152]{1,0:T(8,128)(2,1)}, u32[]{:S(2)}, u32[]{:S(2)}) collective-permute-start(bf16[768,1152]{1,0:T(8,128)(2,1)} %collective-permute-done.2.w_own), channel_id=1, source_target_pairs={{0,16},{16,0},{1,17},{17,1},{2,18},{18,2},{3,19},{19,3},{4,20},{20... | collective-permute-start | bytes 5308424 | tf_op jit(solution)/shard_map/ppermute | solution.py:361
  119.0 147.4 %collective-permute-start.14 = (bf16[1024,768]{1,0:T(8,128)(2,1)}, bf16[1024,768]{1,0:T(8,128)(2,1)}, u32[]{:S(2)}, u32[]{:S(2)}) collective-permute-start(bf16[1024,768]{1,0:T(8,128)(2,1)} %bitcast.11), channel_id=1, source_target_pairs={{0,0},{1,16},{16,1},{17,17},{2,2},{3,18},{18,3},{19,19},{4,4},{5,2... | collective-permute-start | bytes 4718600 | tf_op jit(solution)/shard_map/ppermute | solution.py:357
  122.9 54.7 %collective-permute-start.7 = (bf16[768,384]{1,0:T(8,128)(2,1)}, bf16[768,384]{1,0:T(8,128)(2,1)}, u32[]{:S(2)}, u32[]{:S(2)}) collective-permute-start(bf16[768,384]{1,0:T(8,128)(2,1)} %collective-permute-done.6.out_own), channel_id=1, source_target_pairs={{0,16},{16,0},{1,17},{17,1},{2,18},{18,2},{3,19},{19,3},{4,20},{20... | collective-permute-start | bytes 1769480 | tf_op jit(solution)/shard_map/ppermute | solution.py:361
  124.5 80.4 %collective-permute-start.11 = (bf16[768,1536]{1,0:T(8,128)(2,1)}, bf16[768,1536]{1,0:T(8,128)(2,1)}, u32[]{:S(2)}, u32[]{:S(2)}) collective-permute-start(bf16[768,1536]{1,0:T(8,128)(2,1)} %collective-permute-done.10.down_own), channel_id=1, source_target_pairs={{0,16},{16,0},{1,17},{17,1},{2,18},{18,2},{3,19},{19,3},{4,20},{20... | collective-permute-start | bytes 7077896 | tf_op jit(solution)/shard_map/ppermute | solution.py:361
  318.6 16.5 %collective-permute-start.15 = (bf16[16,10]{1,0:T(8,128)(2,1)S(1)}, bf16[16,10]{1,0:T(8,128)(2,1)S(1)}, u32[]{:S(2)}, u32[]{:S(2)}) collective-permute-start(bf16[16,10]{1,0:T(8,128)(2,1)S(1)} %fusion.38), channel_id=1, source_target_pairs={{1,0},{3,2},{5,4},{7,6},{9,8},{11,10},{13,12},{15,14},{17,16},{19,... | collective-permute-start | bytes 968 | tf_op jit(solution)/shard_map/ppermute | solution.py:482
  329.8 323.7 %collective-permute-start.13 = (bf16[1024,768]{1,0:T(8,128)(2,1)}, bf16[1024,768]{1,0:T(8,128)(2,1)}, u32[]{:S(2)}, u32[]{:S(2)}) collective-permute-start(bf16[1024,768]{1,0:T(8,128)(2,1)} %add_convert_fusion.3), channel_id=1, source_target_pairs={{0,0},{1,16},{16,1},{17,17},{2,2},{3,18},{18,3},{19,19},{4,4},{5,2... | collective-permute-start | bytes 4718600 | tf_op jit(solution)/shard_map/ppermute | solution.py:357
  368.6 125.8 %collective-permute-start.46 = (bf16[768,1536]{1,0:T(8,128)(2,1)}, bf16[768,1536]{1,0:T(8,128)(2,1)}, u32[]{:S(2)}, u32[]{:S(2)}) collective-permute-start(bf16[768,1536]{1,0:T(8,128)(2,1)} %convolution_convert_fusion.4), channel_id=1, source_target_pairs={{0,16},{16,0},{1,17},{17,1},{2,18},{18,2},{3,19},{19,3},{4,20},{20... | collective-permute-start | bytes 7077896 | tf_op jit(solution)/shard_map/ppermute | solution.py:361
  378.6 42.0 %collective-permute-start.28 = (bf16[768,384]{1,0:T(8,128)(2,1)S(1)}, bf16[768,384]{1,0:T(8,128)(2,1)S(1)}, u32[]{:S(2)}, u32[]{:S(2)}) collective-permute-start(bf16[768,384]{1,0:T(8,128)(2,1)S(1)} %convolution_convert_fusion.10), channel_id=1, source_target_pairs={{0,16},{16,0},{1,17},{17,1},{2,18},{18,2},{3,19},{19,3},{4,20},{20... | collective-permute-start | bytes 1769480 | tf_op jit(solution)/shard_map/ppermute | solution.py:361
  412.0 69.7 %collective-permute-start.19 = (bf16[768,1152]{1,0:T(8,128)(2,1)}, bf16[768,1152]{1,0:T(8,128)(2,1)}, u32[]{:S(2)}, u32[]{:S(2)}) collective-permute-start(bf16[768,1152]{1,0:T(8,128)(2,1)} %convolution_convert_fusion.8), channel_id=1, source_target_pairs={{0,16},{16,0},{1,17},{17,1},{2,18},{18,2},{3,19},{19,3},{4,20},{20... | collective-permute-start | bytes 5308424 | tf_op jit(solution)/shard_map/ppermute | solution.py:361
  446.0 69.5 %collective-permute-start.37 = (bf16[768,1536]{1,0:T(8,128)(2,1)}, bf16[768,1536]{1,0:T(8,128)(2,1)}, u32[]{:S(2)}, u32[]{:S(2)}) collective-permute-start(bf16[768,1536]{1,0:T(8,128)(2,1)} %convolution_convert_fusion.6), channel_id=1, source_target_pairs={{0,16},{16,0},{1,17},{17,1},{2,18},{18,2},{3,19},{19,3},{4,20},{20... | collective-permute-start | bytes 7077896 | tf_op jit(solution)/shard_map/ppermute | solution.py:361
  448.0 30.9 %collective-permute-start.34 = (bf16[96,384]{1,0:T(8,128)(2,1)S(1)}, bf16[96,384]{1,0:T(8,128)(2,1)S(1)}, u32[]{:S(2)}, u32[]{:S(2)}) collective-permute-start(bf16[96,384]{1,0:T(8,128)(2,1)S(1)} %get-tuple-element.99), channel_id=1, source_target_pairs={{8,4},{10,6},{12,8},{14,10},{9,5},{11,7},{13,9},{15,11},{24,20},{2... | collective-permute-start | bytes 221192 | tf_op jit(solution)/shard_map/ppermute | solution.py:393
  489.2 134.5 %collective-permute-start.17 = (bf16[16,10]{1,0:T(8,128)(2,1)S(1)}, bf16[16,10]{1,0:T(8,128)(2,1)S(1)}, u32[]{:S(2)}, u32[]{:S(2)}) collective-permute-start(bf16[16,10]{1,0:T(8,128)(2,1)S(1)} %broadcast_select_fusion.3), channel_id=1, source_target_pairs={{0,0},{1,16},{16,1},{17,17},{2,2},{3,18},{18,3},{19,19},{4,4},{5,2... | collective-permute-start | bytes 968 | tf_op jit(solution)/shard_map/ppermute | solution.py:357
  493.9 20.6 %collective-permute-start.20 = (bf16[4,96,1152]{2,1,0:T(8,128)(2,1)S(1)}, bf16[4,96,1152]{2,1,0:T(8,128)(2,1)S(1)}, u32[]{:S(2)}, u32[]{:S(2)}) collective-permute-start(bf16[4,96,1152]{2,1,0:T(8,128)(2,1)S(1)} %dynamic-slice_bitcast_fusion.2), channel_id=1, source_target_pairs={{0,2},{2,0},{4,6},{6,4},{8,10},{10,8},{12,14},{14,12},{1,3},{3,1},... | collective-permute-start | bytes 2654216 | tf_op jit(solution)/shard_map/ppermute | solution.py:382
  494.4 159.1 %collective-permute-start.16 = (bf16[1024,768]{1,0:T(8,128)(2,1)S(1)}, bf16[1024,768]{1,0:T(8,128)(2,1)S(1)}, u32[]{:S(2)}, u32[]{:S(2)}) collective-permute-start(bf16[1024,768]{1,0:T(8,128)(2,1)S(1)} %copy-done.8), channel_id=1, source_target_pairs={{0,0},{1,16},{16,1},{17,17},{2,2},{3,18},{18,3},{19,19},{4,4},{5,2... | collective-permute-start | bytes 4718600 | tf_op jit(solution)/shard_map/ppermute | solution.py:357
  526.7 26.8 %collective-permute-start.47 = (bf16[4,96,1536]{2,1,0:T(8,128)(2,1)S(1)}, bf16[4,96,1536]{2,1,0:T(8,128)(2,1)S(1)}, u32[]{:S(2)}, u32[]{:S(2)}) collective-permute-start(bf16[4,96,1536]{2,1,0:T(8,128)(2,1)S(1)} %dynamic-slice_bitcast_fusion), channel_id=1, source_target_pairs={{0,2},{2,0},{4,6},{6,4},{8,10},{10,8},{12,14},{14,12},{1,3},{3,1},... | collective-permute-start | bytes 3538952 | tf_op jit(solution)/shard_map/ppermute | solution.py:382
  538.7 40.0 %collective-permute-start.38 = (bf16[4,96,1536]{2,1,0:T(8,128)(2,1)S(1)}, bf16[4,96,1536]{2,1,0:T(8,128)(2,1)S(1)}, u32[]{:S(2)}, u32[]{:S(2)}) collective-permute-start(bf16[4,96,1536]{2,1,0:T(8,128)(2,1)S(1)} %dynamic-slice_bitcast_fusion.1), channel_id=1, source_target_pairs={{0,2},{2,0},{4,6},{6,4},{8,10},{10,8},{12,14},{14,12},{1,3},{3,1},... | collective-permute-start | bytes 3538952 | tf_op jit(solution)/shard_map/ppermute | solution.py:382
  553.8 26.6 %collective-permute-start.48 = (bf16[96,1536]{1,0:T(8,128)(2,1)S(1)}, bf16[96,1536]{1,0:T(8,128)(2,1)S(1)}, u32[]{:S(2)}, u32[]{:S(2)}) collective-permute-start(bf16[96,1536]{1,0:T(8,128)(2,1)S(1)} %get-tuple-element.88), channel_id=1, source_target_pairs={{0,4},{2,6},{1,5},{3,7},{16,20},{18,22},{17,21},{19,23}} | collective-permute-start | bytes 884744 | tf_op jit(solution)/shard_map/ppermute | solution.py:389
  616.2 20.0 %collective-permute-start.41 = (bf16[96,1536]{1,0:T(8,128)(2,1)S(1)}, bf16[96,1536]{1,0:T(8,128)(2,1)S(1)}, u32[]{:S(2)}, u32[]{:S(2)}) collective-permute-start(bf16[96,1536]{1,0:T(8,128)(2,1)S(1)} %get-tuple-element.90), channel_id=1, source_target_pairs={{0,4},{2,6},{4,8},{6,10},{8,12},{10,14},{1,5},{3,7},{5,9},{7,11},{... | collective-permute-start | bytes 884744 | tf_op jit(solution)/shard_map/ppermute | solution.py:389
  619.9 18.2 %collective-permute-start.44 = (bf16[96,1536]{1,0:T(8,128)(2,1)S(1)}, bf16[96,1536]{1,0:T(8,128)(2,1)S(1)}, u32[]{:S(2)}, u32[]{:S(2)}) collective-permute-start(bf16[96,1536]{1,0:T(8,128)(2,1)S(1)} %fusion.19), channel_id=1, source_target_pairs={{4,0},{6,2},{8,4},{10,6},{12,8},{14,10},{5,1},{7,3},{9,5},{11,7},{... | collective-permute-start | bytes 884744 | tf_op jit(solution)/shard_map/ppermute | solution.py:393
  623.7 18.0 %collective-permute-start.18 = (f32[2,768]{1,0:T(2,128)S(1)}, f32[2,768]{1,0:T(2,128)S(1)}, u32[]{:S(2)}, u32[]{:S(2)}) collective-permute-start(f32[2,768]{1,0:T(2,128)S(1)} %psum.7), channel_id=1, source_target_pairs={{0,0},{1,16},{16,1},{17,17},{2,2},{3,18},{18,3},{19,19},{4,4},{5,2... | collective-permute-start | bytes 18440 | tf_op jit(solution)/shard_map/ppermute | solution.py:357
  644.8 23.2 %collective-permute-start.54 = (f32[96,1536]{1,0:T(8,128)S(1)}, f32[96,1536]{1,0:T(8,128)S(1)}, u32[]{:S(2)}, u32[]{:S(2)}) collective-permute-start(f32[96,1536]{1,0:T(8,128)S(1)} %fusion.17), channel_id=1, source_target_pairs={{0,0},{1,16},{16,1},{17,17},{2,2},{3,18},{18,3},{19,19},{4,4},{5,2... | collective-permute-start | bytes 1769480 | tf_op jit(solution)/shard_map/ppermute | solution.py:357
  647.2 20.8 %collective-permute-start.45 = (f32[96,1536]{1,0:T(8,128)S(1)}, f32[96,1536]{1,0:T(8,128)S(1)}, u32[]{:S(2)}, u32[]{:S(2)}) collective-permute-start(f32[96,1536]{1,0:T(8,128)S(1)} %fusion.22), channel_id=1, source_target_pairs={{0,0},{1,16},{16,1},{17,17},{2,2},{3,18},{18,3},{19,19},{4,4},{5,2... | collective-permute-start | bytes 1769480 | tf_op jit(solution)/shard_map/ppermute | solution.py:357
  650.5 16.6 %collective-permute-start.27 = (f32[96,1152]{1,0:T(8,128)S(1)}, f32[96,1152]{1,0:T(8,128)S(1)}, u32[]{:S(2)}, u32[]{:S(2)}) collective-permute-start(f32[96,1152]{1,0:T(8,128)S(1)} %fusion.28), channel_id=1, source_target_pairs={{0,0},{1,16},{16,1},{17,17},{2,2},{3,18},{18,3},{19,19},{4,4},{5,2... | collective-permute-start | bytes 1327112 | tf_op jit(solution)/shard_map/ppermute | solution.py:357
  (46 other events, 505.8 us)
